TPU v7x, 128 devices: a whole 4x4x4 slice. The times are simulated.
128 devices in a mesh: dp: 16 (over y, z), expert: 8 (over x, core).
Axes of the slice: x: 4, y: 4, z: 4, core: 2. Of those that a mesh axis runs over, the one named last changes fastest.
Arguments:
- grad_out: bfloat16 [16384, 6144], P(('dp', 'expert')), may hold values from -6 to 6
- routes: int32 [16384, 2], P(('dp', 'expert')), may hold values from 0 to 31, all different within a row; in each aligned block of 128 rows (0 to 127, 128 to 255, ...) at most 9 rows name the same one
- loss_weight: int32 [16384], P(('dp', 'expert')), may hold values from 1 to 4
- saved_input: bfloat16 [32, 1152, 6144], P('dp', None, 'expert'), may hold values from -6 to 6
- saved_gate: bfloat16 [32, 1152, 1024], P('dp', None, 'expert'), may hold values from -8 to 8
- saved_up: bfloat16 [32, 1152, 1024], P('dp', None, 'expert'), may hold values from -6 to 6
- w_gate: bfloat16 [32, 6144, 1024], P('dp', 'expert'), may hold values from -0.1875 to 0.1875
- w_up: bfloat16 [32, 6144, 1024], P('dp', 'expert'), may hold values from -0.1875 to 0.1875
- w_down: bfloat16 [32, 1024, 6144], P('dp', None, 'expert'), may hold values from -0.078125 to 0.078125
Outputs:
- grad_input: bfloat16 [16384, 6144], P(('dp', 'expert'))
- grad_gate: bfloat16 [32, 6144, 1024], P('dp', 'expert')
- grad_up: bfloat16 [32, 6144, 1024], P('dp', 'expert')
- grad_down: bfloat16 [32, 1024, 6144], P('dp', None, 'expert')
Inputs may be any that keep to these rules, and one draw needn't show every extreme that they name: `routes`: each row names two different experts; among the rows of one device no expert is named more than 9 times, and some device names some expert exactly 9 times.
All inputs are finite; a program needn't handle non-finite values.
Results may differ from a plain program's by a relative error of at most 0.0061.
Values may be sent and summed in bfloat16 or wider, within the bound.
No kernel may reach another device: no remote copies, remote signals or barrier semaphores. Data moves between devices by JAX's collectives and lax.ppermute only.
A program may use at most 192 MiB of HBM per device.

v0:
```python
import jax
import jax.numpy as jnp
from jax import lax
from jax.sharding import PartitionSpec as P


def body(grad_out, routes, loss_weight, saved_input, saved_gate, saved_up, w_gate, w_up, w_down):
    groups = lax.axis_size("dp")
    splits = lax.axis_size("expert")
    local_experts = w_gate.shape[0]
    experts_all = local_experts * groups
    tokens_here = grad_out.shape[0]
    width = grad_out.shape[1]
    slice_width = width // splits
    slots_all = saved_input.shape[1]
    capacity = slots_all // (groups * splits)
    scaled = (
        grad_out.astype(jnp.float32) * loss_weight.astype(jnp.float32)[:, None] * 0.25
    ).astype(jnp.bfloat16)
    chosen = routes.reshape(-1)
    onehot = (chosen[:, None] == jnp.arange(experts_all, dtype=jnp.int32)[None, :]).astype(
        jnp.int32
    )
    before = jnp.cumsum(onehot, axis=0) - onehot
    rank = jnp.sum(before * onehot, axis=1)
    dest_row = (chosen % local_experts * groups + chosen // local_experts) * capacity + rank
    marks = (
        dest_row[:, None] == jnp.arange(experts_all * capacity, dtype=jnp.int32)[None, :]
    ).astype(jnp.float32)
    placed = jnp.sum(marks.reshape(tokens_here, 2, experts_all * capacity), axis=1).astype(
        jnp.bfloat16
    )
    outgoing = jnp.einsum("tr,td->rd", placed, scaled, preferred_element_type=jnp.float32).astype(
        jnp.bfloat16
    )
    ordered = outgoing.reshape(local_experts, groups, capacity, splits, slice_width)
    ordered = ordered.transpose(0, 1, 3, 2, 4).reshape(
        local_experts, groups * splits, capacity, slice_width
    )
    arrived = lax.all_to_all(ordered, ("dp", "expert"), split_axis=1, concat_axis=1, tiled=True)
    dispatched = arrived.reshape(local_experts, slots_all, slice_width)
    partial_value = jnp.einsum(
        "esd,ehd->esh", dispatched, w_down, preferred_element_type=jnp.float32
    )
    dhidden = lax.psum(partial_value, "expert")
    gates_all, ups_all = (
        lax.all_gather(saved_gate, "expert", axis=2, tiled=True),
        lax.all_gather(saved_up, "expert", axis=2, tiled=True),
    )
    gvals = gates_all.astype(jnp.float32)
    uvals = ups_all.astype(jnp.float32)
    sig = jax.nn.sigmoid(gvals)
    act = gvals * sig
    hidden = (act * uvals).astype(jnp.bfloat16)
    dgate = (dhidden * uvals * sig * (1.0 + gvals * (1.0 - sig))).astype(jnp.bfloat16)
    dup = (dhidden * act).astype(jnp.bfloat16)
    hidden, dgate, dup = (hidden, dgate, dup)
    grad_down = jnp.einsum(
        "esh,esd->ehd", hidden, dispatched, preferred_element_type=jnp.float32
    ).astype(jnp.bfloat16)
    grad_gate = jnp.einsum(
        "esd,esh->edh", saved_input, dgate, preferred_element_type=jnp.float32
    ).astype(jnp.bfloat16)
    grad_up = jnp.einsum(
        "esd,esh->edh", saved_input, dup, preferred_element_type=jnp.float32
    ).astype(jnp.bfloat16)
    slot_grad = jnp.einsum("esh,edh->esd", dgate, w_gate, preferred_element_type=jnp.float32)
    slot_grad = slot_grad + jnp.einsum(
        "esh,edh->esd", dup, w_up, preferred_element_type=jnp.float32
    )
    slot_grad = slot_grad.astype(jnp.bfloat16)
    leaving = slot_grad.reshape(local_experts, groups * splits, capacity, slice_width)
    returned = lax.all_to_all(leaving, ("dp", "expert"), split_axis=1, concat_axis=1, tiled=True)
    returned = returned.reshape(local_experts, groups, splits, capacity, slice_width).transpose(
        0, 1, 3, 2, 4
    )
    returned = returned.reshape(experts_all * capacity, width)
    grad_input = jnp.einsum(
        "tr,rd->td", placed, returned, preferred_element_type=jnp.float32
    ).astype(jnp.bfloat16)
    return (grad_input, grad_gate, grad_up, grad_down)


def solution(mesh):
    return jax.shard_map(
        body,
        mesh=mesh,
        in_specs=(
            P(("dp", "expert"), None),
            P(("dp", "expert"), None),
            P(("dp", "expert")),
            P("dp", None, "expert"),
            P("dp", None, "expert"),
            P("dp", None, "expert"),
            P("dp", "expert", None),
            P("dp", "expert", None),
            P("dp", None, "expert"),
        ),
        out_specs=(
            P(("dp", "expert"), None),
            P("dp", "expert", None),
            P("dp", "expert", None),
            P("dp", None, "expert"),
        ),
        check_vma=False,
    )
```

profile of v0, /device:TPU:1, one launch (start us, length us, event | category | flops | bytes accessed | tf_op | source)
XLA Modules:
  0.0 385.4 jit_solution(1867682180642988697)
XLA Ops:
  7.2 1.6 copy.105
  8.8 1.0 eq.45
  9.8 1.0 eq.41
  12.0 1.9 reduce-window.6
  13.9 0.9 slice_reduce_fusion
  14.9 0.9 fusion.24
  15.8 0.8 reduce_sum.21
  16.5 0.9 copy.108
  17.4 0.7 multiply_add_fusion
  18.2 2.6 convolution_convert_fusion
  20.8 1.0 copy.124
  22.3 3.6 copy.110
  25.9 57.3 %all_to_all.10 = bf16[2,128,9,768]{3,0,2,1:T(2,128)(2,1)S(1)} all-to-all(bf16[2,128,9,768]{3,0,2,1:T(2,128)(2,1)S(1)} %copy.110), channel_id=1, replica_groups=mesh['dp'=16,'expert'=8] {'dp','expert'}, dimensions={1} | all-to-all | bytes 7077888 | tf_op jit(solution)/shard_map/all_to_all | solution.py:40
  83.3 1.9 copy-done.3
  85.1 6.2 %fusion.11 = f32[2,1152,1024]{2,1,0:T(8,128)} fusion(bf16[2,1024,768]{2,1,0:T(8,128)(2,1)S(1)} %copy-done.6, bf16[2,1152,768]{2,0,1:T(2,128)(2,1)S(1)} %bitcast.56), kind=kOutput, calls=%fused_computation.23 | convolution fusion | flops 3623878656 | bytes 16121856 | tf_op jit(solution)/shard_map/esd,ehd->esh/dot_general | solution.py:42
  92.8 108.4 %all-reduce.2.cloned.1.call-done = f32[2,1152,1024]{2,1,0:T(8,128)} async-done(((f32[2,1152,1024]{2,1,0:T(8,128)}), f32[2,1152,1024]{2,1,0:T(8,128)}) %all-reduce.2.cloned.1.call-update) | async-done | bytes 9437200 | tf_op jit(solution)/shard_map/psum | solution.py:45
  201.2 40.5 %all-gather.5.cloned.1.call-done = bf16[2,1152,1024]{2,1,0:T(8,128)(2,1)} async-done(((bf16[2,1152,128]{2,1,0:T(8,128)(2,1)}), bf16[2,1152,1024]{2,1,0:T(8,128)(2,1)}) %all-gather.5.cloned.1.call-update) | async-done | bytes 4718608 | tf_op jit(solution)/shard_map/all_gather | solution.py:47
  241.8 41.0 %all-gather.3.cloned.1.call-done = bf16[2,1152,1024]{2,1,0:T(8,128)(2,1)} async-done(((bf16[2,1152,128]{2,1,0:T(8,128)(2,1)}), bf16[2,1152,1024]{2,1,0:T(8,128)(2,1)}) %all-gather.3.cloned.1.call-update) | async-done | bytes 4718608 | tf_op jit(solution)/shard_map/all_gather | solution.py:48
  282.7 9.0 %multiply_convert_fusion = (bf16[2,1152,1024]{2,1,0:T(8,128)(2,1)S(1)}, bf16[2,1152,1024]{2,1,0:T(8,128)(2,1)S(1)}) fusion(f32[2,1152,1024]{2,1,0:T(8,128)} %all-reduce.2.cloned.1.call-done, bf16[2,1152,1024]{2,1,0:T(8,128)(2,1)} %all-gather.5.cloned.1.call-done, bf16[2,1152,1024]{2,1,0:T(8,128)(2,1)} %all-gather.3.cloned.1.call-done), kind=kLoop, calls=%fused_computation.13 | loop fusion | flops 35389440 | bytes 28311552 | tf_op jit(solution)/shard_map/convert_element_type | solution.py:56
  291.8 5.9 %fusion.30 = f32[2,1152,768]{2,1,0:T(8,128)} fusion(bf16[2,1152,1024]{2,1,0:T(8,128)(2,1)S(1)} %get-tuple-element.29, bf16[2,768,1024]{2,1,0:T(8,128)(2,1)S(1)} %copy-done.7), kind=kOutput, calls=%fused_computation.51 | convolution fusion | flops 3623878656 | bytes 14942208 | tf_op jit(solution)/shard_map/esh,edh->esd/dot_general | solution.py:67
  298.2 6.1 %add_convert_fusion = bf16[2,1152,768]{2,1,0:T(8,128)(2,1)S(1)} fusion(f32[2,1152,768]{2,1,0:T(8,128)} %fusion.30, bf16[2,1152,1024]{2,1,0:T(8,128)(2,1)S(1)} %get-tuple-element.28, bf16[2,768,1024]{2,1,0:T(8,128)(2,1)S(1)} %copy-done.8), kind=kOutput, calls=%fused_computation.16 | convolution fusion | flops 3627417600 | bytes 18481152 | tf_op jit(solution)/shard_map/esh,edh->esd/dot_general | solution.py:68
  304.3 13.9 %copy.112 = bf16[2,1152,768]{2,0,1:T(2,128)(2,1)} copy(bf16[2,1152,768]{2,1,0:T(8,128)(2,1)S(1)} %add_convert_fusion) | data formatting | bytes 7077888 | tf_op jit(solution)/shard_map/convert_element_type | solution.py:71
  318.2 9.3 %all-to-all-start.1 = ((bf16[2,128,9,768]{3,0,2,1:T(2,128)(2,1)}), bf16[2,128,9,768]{3,0,2,1:T(2,128)(2,1)}, u32[]{:S(2)}, u32[]{:S(2)}) async-start(bf16[2,128,9,768]{3,0,2,1:T(2,128)(2,1)} %bitcast.52), calls=%async_computation.1 | async-start | bytes 7077888 | tf_op jit(solution)/shard_map/all_to_all | solution.py:73
  327.5 9.4 %convert_bitcast_fusion = bf16[2,768,1024]{1,2,0:T(8,128)(2,1)} fusion(bf16[2,1152,1024]{2,1,0:T(8,128)(2,1)} %copy-done.2, bf16[2,1152,768]{2,1,0:T(8,128)(2,1)S(1)} %copy-done), kind=kOutput, calls=%fused_computation.19 | convolution fusion | flops 3625451520 | bytes 11403264 | tf_op jit(solution)/shard_map/esd,esh->edh/dot_general | solution.py:64
  337.0 4.6 %copy.119 = bf16[2,768,1024]{2,1,0:T(8,128)(2,1)} copy(bf16[2,768,1024]{1,2,0:T(8,128)(2,1)} %convert_bitcast_fusion) | data formatting | bytes 6291456
  341.6 9.4 %convert_bitcast_fusion.1 = bf16[2,768,1024]{1,2,0:T(8,128)(2,1)} fusion(bf16[2,1152,1024]{2,1,0:T(8,128)(2,1)} %copy-done.1, bf16[2,1152,768]{2,1,0:T(8,128)(2,1)S(1)} %copy-done), kind=kOutput, calls=%fused_computation.20 | convolution fusion | flops 3625451520 | bytes 11403264 | tf_op jit(solution)/shard_map/esd,esh->edh/dot_general | solution.py:61
  351.0 4.6 %copy.118 = bf16[2,768,1024]{2,1,0:T(8,128)(2,1)} copy(bf16[2,768,1024]{1,2,0:T(8,128)(2,1)} %convert_bitcast_fusion.1) | data formatting | bytes 6291456
  355.6 12.1 %fusion.13 = bf16[2,1024,768]{2,1,0:T(8,128)(2,1)} fusion(bf16[2,1152,768]{2,0,1:T(2,128)(2,1)} %bitcast.57, bf16[2,1152,1024]{2,1,0:T(8,128)(2,1)} %all-gather.3.cloned.1.call-done, bf16[2,1152,1024]{2,1,0:T(8,128)(2,1)} %all-gather.5.cloned.1.call-done), kind=kOutput, calls=%fused_computation.25 | convolution fusion | flops 3644325888 | bytes 16121856 | tf_op jit(solution)/shard_map/esh,esd->ehd/dot_general | solution.py:58
  367.8 5.5 %all-to-all-done.1 = bf16[2,128,9,768]{3,0,2,1:T(2,128)(2,1)} async-done(((bf16[2,128,9,768]{3,0,2,1:T(2,128)(2,1)}), bf16[2,128,9,768]{3,0,2,1:T(2,128)(2,1)}, u32[]{:S(2)}, u32[]{:S(2)}) %all-to-all-start.1) | async-done | bytes 3538976 | tf_op jit(solution)/shard_map/all_to_all | solution.py:73
  373.2 2.5 copy.113
  375.7 1.0 copy.125
  376.7 2.2 convolution_convert_fusion.1
  (29 shorter events, 3.7 us)
Async XLA Ops:
  7.2 320.4 %copy-start = (bf16[2,1152,768]{2,1,0:T(8,128)(2,1)S(1)}, bf16[2,1152,768]{2,1,0:T(8,128)(2,1)}, u32[]{:S(2)}) copy-start(bf16[2,1152,768]{2,1,0:T(8,128)(2,1)} %param.12) | copy-start | bytes 10616836
  7.2 194.1 %all-reduce.2.cloned.1.call-start = ((), (), s32[]{:S(2)}) async-start(), calls=%async_computation.2 | async-start | bytes 18874368 | tf_op jit(solution)/shard_map/psum | solution.py:45
  18.2 2.6 copy-start.4
  25.9 59.2 %copy-start.6 = (bf16[2,1024,768]{2,1,0:T(8,128)(2,1)S(1)}, bf16[2,1024,768]{2,1,0:T(8,128)(2,1)}, u32[]{:S(2)}) copy-start(bf16[2,1024,768]{2,1,0:T(8,128)(2,1)} %param.17) | copy-start | bytes 9437188
  83.2 1.9 copy-start.3
  91.3 150.4 %all-gather.5.cloned.1.call-start = ((), (), s32[]{:S(2)}) async-start(), calls=%async_computation.4 | async-start | bytes 5308416 | tf_op jit(solution)/shard_map/all_gather | solution.py:47
  92.1 190.6 %all-gather.3.cloned.1.call-start = ((), (), s32[]{:S(2)}) async-start(), calls=%async_computation.3 | async-start | bytes 5308416 | tf_op jit(solution)/shard_map/all_gather | solution.py:48
  282.7 9.1 %copy-start.7 = (bf16[2,768,1024]{2,1,0:T(8,128)(2,1)S(1)}, bf16[2,768,1024]{2,1,0:T(8,128)(2,1)}, u32[]{:S(2)}) copy-start(bf16[2,768,1024]{2,1,0:T(8,128)(2,1)} %param.15) | copy-start | bytes 9437188
  291.8 6.0 %copy-start.1 = (bf16[2,1152,1024]{2,1,0:T(8,128)(2,1)}, bf16[2,1152,1024]{2,1,0:T(8,128)(2,1)S(1)}, u32[]{:S(2)}) copy-start(bf16[2,1152,1024]{2,1,0:T(8,128)(2,1)S(1)} %get-tuple-element.29) | copy-start | bytes 14155780
  291.8 6.4 %copy-start.2 = (bf16[2,1152,1024]{2,1,0:T(8,128)(2,1)}, bf16[2,1152,1024]{2,1,0:T(8,128)(2,1)S(1)}, u32[]{:S(2)}) copy-start(bf16[2,1152,1024]{2,1,0:T(8,128)(2,1)S(1)} %get-tuple-element.28) | copy-start | bytes 14155780
  291.8 6.4 %copy-start.8 = (bf16[2,768,1024]{2,1,0:T(8,128)(2,1)S(1)}, bf16[2,768,1024]{2,1,0:T(8,128)(2,1)}, u32[]{:S(2)}) copy-start(bf16[2,768,1024]{2,1,0:T(8,128)(2,1)} %param.16) | copy-start | bytes 9437188
  318.2 55.0 %all-to-all-start.1 = ((bf16[2,128,9,768]{3,0,2,1:T(2,128)(2,1)}), bf16[2,128,9,768]{3,0,2,1:T(2,128)(2,1)}, u32[]{:S(2)}, u32[]{:S(2)}) async-start(bf16[2,128,9,768]{3,0,2,1:T(2,128)(2,1)} %bitcast.52), calls=%async_computation.1 | async-start | bytes 7077888 | tf_op jit(solution)/shard_map/all_to_all | solution.py:73
  375.7 1.0 copy-start.5
Sparse Core Ops, SparseCore 0:
  91.5 109.7 all-reduce.1
  202.9 38.8 all-gather.4
  243.5 39.2 all-gather.2
where the time goes:
time: 386 us; the launch traced here: 385 us
  waiting for transfers between devices  197 us (51%)
  blocking collectives  57.3 us (15%)
  matrix products  54 us (14%)
  local copies, waits for them, and re-layouts  40.1 us (10%)
  other arithmetic  13.9 us (4%)
  between operations  13.9 us (4%)
  starting transfers between devices  9.56 us (2%)
    psum x1, waiting for transfers between devices, body(): dhidden = lax.psum(partial_value, 'expert')  108 us
    all_to_all x1, blocking collectives, body(): lax.all_to_all(ordered, ('dp', 'expert'), split_axis=1, concat_axis=1, ti...  57.3 us
    all_gather x1, waiting for transfers between devices, body(): lax.all_gather(saved_up, 'expert', axis=2, tiled=True)  41 us
    all_gather x1, waiting for transfers between devices, body(): lax.all_gather(saved_gate, 'expert', axis=2, tiled=True)  40.5 us
    unnamed x23, local copies, waits for them, and re-layouts  15.2 us
    convert_element_type x1, local copies, waits for them, and re-layouts, body(): slot_grad = slot_grad.astype(jnp.bfloat16)  13.9 us
    dot_general x1, matrix products, body(): jnp.einsum('esh,esd->ehd', hidden, dispatched, preferred_element_type=jnp...  12.1 us
    dot_general x1, matrix products, body(): jnp.einsum('esd,esh->edh', saved_input, dup, preferred_element_type=jnp.f...  9.43 us
  transfers between devices with their start and end apart: 4, of which 4 were waited for; matrix products, arithmetic and copies ran while one was open for 10% of the time, Pallas kernels for 0%

commit v1 on v0

--- a/solution.py
+++ b/solution.py
@@ -44,7 +44,10 @@
     )
     dhidden = lax.psum(partial_value, "expert")
     gates_all, ups_all = (
-        lax.all_gather(saved_gate, "expert", axis=2, tiled=True),
+        jnp.concatenate(
+            lax.all_to_all(jnp.stack([saved_gate] * lax.axis_size("expert")), "expert", 0, 0),
+            axis=2,
+        ),
         lax.all_gather(saved_up, "expert", axis=2, tiled=True),
     )
     gvals = gates_all.astype(jnp.float32)

time: 386 us -> 395 us (1.023)
  blocking collectives: 57.3 us -> 141 us
  waiting for transfers between devices: 197 us -> 119 us
    all_to_all x0 -> x1, blocking collectives: none -> 84.1 us  [body(): lax.all_to_all(jnp.stack([saved_gate] * lax.axis_size('expert')), 'expert...]
    all_gather x1 -> x0, waiting for transfers between devices: 40.5 us -> none  [body(): lax.all_gather(saved_gate, 'expert', axis=2, tiled=True)]
    psum x1, waiting for transfers between devices: 108 us -> 72 us  [body(): dhidden = lax.psum(partial_value, 'expert')]
  transfers between devices with their start and end apart: 4 -> 3, of which waited for: 4 -> 3; matrix products, arithmetic and copies ran while one was open for 10% -> 11% of each run, Pallas kernels for 0% -> 0%
where the time goes in v1:
time: 395 us; the launch traced here: 394 us
  blocking collectives  141 us (36%)
  waiting for transfers between devices  119 us (30%)
  matrix products  54 us (14%)
  local copies, waits for them, and re-layouts  42.1 us (11%)
  between operations  14.2 us (4%)
  other arithmetic  13.9 us (4%)
  starting transfers between devices  9.34 us (2%)
    all_to_all x1, blocking collectives, body(): lax.all_to_all(jnp.stack([saved_gate] * lax.axis_size('expert')), 'expert...  84.1 us
    psum x1, waiting for transfers between devices, body(): dhidden = lax.psum(partial_value, 'expert')  72 us
    all_to_all x1, blocking collectives, body(): lax.all_to_all(ordered, ('dp', 'expert'), split_axis=1, concat_axis=1, ti...  57.3 us
    all_gather x1, waiting for transfers between devices, body(): lax.all_gather(saved_up, 'expert', axis=2, tiled=True)  40.5 us
    unnamed x23, local copies, waits for them, and re-layouts  15.2 us
    convert_element_type x1, local copies, waits for them, and re-layouts, body(): slot_grad = slot_grad.astype(jnp.bfloat16)  13.9 us
    dot_general x1, matrix products, body(): jnp.einsum('esh,esd->ehd', hidden, dispatched, preferred_element_type=jnp...  12.1 us
    dot_general x1, matrix products, body(): jnp.einsum('esd,esh->edh', saved_input, dup, preferred_element_type=jnp.f...  9.43 us
  transfers between devices with their start and end apart: 3, of which 3 were waited for; matrix products, arithmetic and copies ran while one was open for 11% of the time, Pallas kernels for 0%

profile of v1, /device:TPU:1, one launch (start us, length us, event | category | flops | bytes accessed | tf_op | source)
XLA Modules:
  0.0 393.7 jit_solution(14988881456168106648)
XLA Ops:
  7.2 1.6 copy.108
  8.8 1.0 eq.45
  9.8 1.0 eq.41
  12.0 1.9 reduce-window.6
  13.9 0.9 slice_reduce_fusion
  14.9 0.9 fusion.24
  15.8 0.8 reduce_sum.21
  16.5 0.9 copy.111
  18.2 2.6 convolution_convert_fusion
  20.8 1.0 copy.129
  22.3 3.6 copy.113
  25.9 57.3 %all_to_all.15 = bf16[2,128,9,768]{3,0,2,1:T(2,128)(2,1)S(1)} all-to-all(bf16[2,128,9,768]{3,0,2,1:T(2,128)(2,1)S(1)} %copy.113), channel_id=1, replica_groups=mesh['dp'=16,'expert'=8] {'dp','expert'}, dimensions={1} | all-to-all | bytes 7077888 | tf_op jit(solution)/shard_map/all_to_all | solution.py:40
  83.3 1.9 copy-done.3
  85.1 6.2 %fusion.11 = f32[2,1152,1024]{2,1,0:T(8,128)} fusion(bf16[2,1024,768]{2,1,0:T(8,128)(2,1)S(1)} %copy-done.6, bf16[2,1152,768]{2,0,1:T(2,128)(2,1)S(1)} %bitcast.85), kind=kOutput, calls=%fused_computation.24 | convolution fusion | flops 3623878656 | bytes 16121856 | tf_op jit(solution)/shard_map/esd,ehd->esh/dot_general | solution.py:42
  92.1 2.0 stack.2
  94.1 84.1 %all_to_all.16 = bf16[8,2,1152,128]{3,2,1,0:T(8,128)(2,1)} all-to-all(bf16[8,2,1152,128]{3,2,1,0:T(8,128)(2,1)S(1)} %stack.2), channel_id=1, replica_groups=mesh['dp'=16,'expert'=8] {'expert'}, dimensions={0} | all-to-all | bytes 9437184 | tf_op jit(solution)/shard_map/all_to_all | solution.py:48
  178.2 72.0 %all-reduce.2.cloned.1.call-done = f32[2,1152,1024]{2,1,0:T(8,128)} async-done(((f32[2,1152,1024]{2,1,0:T(8,128)}), f32[2,1152,1024]{2,1,0:T(8,128)}) %all-reduce.2.cloned.1.call-update) | async-done | bytes 9437200 | tf_op jit(solution)/shard_map/psum | solution.py:45
  250.1 40.5 %all-gather.2.cloned.1.call-done = bf16[2,1152,1024]{2,1,0:T(8,128)(2,1)} async-done(((bf16[2,1152,128]{2,1,0:T(8,128)(2,1)}), bf16[2,1152,1024]{2,1,0:T(8,128)(2,1)}) %all-gather.2.cloned.1.call-update) | async-done | bytes 4718608 | tf_op jit(solution)/shard_map/all_gather | solution.py:51
  290.7 9.0 %multiply_convert_fusion = (bf16[2,1152,1024]{2,1,0:T(8,128)(2,1)S(1)}, bf16[2,1152,1024]{2,1,0:T(8,128)(2,1)S(1)}) fusion(f32[2,1152,1024]{2,1,0:T(8,128)} %all-reduce.2.cloned.1.call-done, bf16[2,1152,1024]{2,1,0:T(8,128)(2,1)} %all-gather.2.cloned.1.call-done, bf16[8,2,1152,128]{3,2,1,0:T(8,128)(2,1)} %all_to_all.16), kind=kLoop, calls=%fused_computation.14 | loop fusion | flops 35389440 | bytes 28311552 | tf_op jit(solution)/shard_map/convert_element_type | solution.py:59
  299.8 5.9 %fusion.30 = f32[2,1152,768]{2,1,0:T(8,128)} fusion(bf16[2,1152,1024]{2,1,0:T(8,128)(2,1)S(1)} %get-tuple-element.29, bf16[2,768,1024]{2,1,0:T(8,128)(2,1)S(1)} %copy-done.7), kind=kOutput, calls=%fused_computation.52 | convolution fusion | flops 3623878656 | bytes 14942208 | tf_op jit(solution)/shard_map/esh,edh->esd/dot_general | solution.py:70
  306.1 6.1 %add_convert_fusion = bf16[2,1152,768]{2,1,0:T(8,128)(2,1)S(1)} fusion(f32[2,1152,768]{2,1,0:T(8,128)} %fusion.30, bf16[2,1152,1024]{2,1,0:T(8,128)(2,1)S(1)} %get-tuple-element.28, bf16[2,768,1024]{2,1,0:T(8,128)(2,1)S(1)} %copy-done.8), kind=kOutput, calls=%fused_computation.17 | convolution fusion | flops 3627417600 | bytes 18481152 | tf_op jit(solution)/shard_map/esh,edh->esd/dot_general | solution.py:71
  312.2 13.9 %copy.116 = bf16[2,1152,768]{2,0,1:T(2,128)(2,1)} copy(bf16[2,1152,768]{2,1,0:T(8,128)(2,1)S(1)} %add_convert_fusion) | data formatting | bytes 7077888 | tf_op jit(solution)/shard_map/convert_element_type | solution.py:74
  326.2 9.3 %all-to-all-start.2 = ((bf16[2,128,9,768]{3,0,2,1:T(2,128)(2,1)}), bf16[2,128,9,768]{3,0,2,1:T(2,128)(2,1)}, u32[]{:S(2)}, u32[]{:S(2)}) async-start(bf16[2,128,9,768]{3,0,2,1:T(2,128)(2,1)} %bitcast.81), calls=%async_computation.2 | async-start | bytes 7077888 | tf_op jit(solution)/shard_map/all_to_all | solution.py:76
  335.5 9.4 %convert_bitcast_fusion.1 = bf16[2,768,1024]{1,2,0:T(8,128)(2,1)} fusion(bf16[2,1152,1024]{2,1,0:T(8,128)(2,1)} %copy-done.2, bf16[2,1152,768]{2,1,0:T(8,128)(2,1)S(1)} %copy-done), kind=kOutput, calls=%fused_computation.20 | convolution fusion | flops 3625451520 | bytes 11403264 | tf_op jit(solution)/shard_map/esd,esh->edh/dot_general | solution.py:67
  344.9 4.6 %copy.123 = bf16[2,768,1024]{2,1,0:T(8,128)(2,1)} copy(bf16[2,768,1024]{1,2,0:T(8,128)(2,1)} %convert_bitcast_fusion.1) | data formatting | bytes 6291456
  349.5 9.4 %convert_bitcast_fusion.2 = bf16[2,768,1024]{1,2,0:T(8,128)(2,1)} fusion(bf16[2,1152,1024]{2,1,0:T(8,128)(2,1)} %copy-done.1, bf16[2,1152,768]{2,1,0:T(8,128)(2,1)S(1)} %copy-done), kind=kOutput, calls=%fused_computation.21 | convolution fusion | flops 3625451520 | bytes 11403264 | tf_op jit(solution)/shard_map/esd,esh->edh/dot_general | solution.py:64
  359.0 4.6 %copy.122 = bf16[2,768,1024]{2,1,0:T(8,128)(2,1)} copy(bf16[2,768,1024]{1,2,0:T(8,128)(2,1)} %convert_bitcast_fusion.2) | data formatting | bytes 6291456
  363.6 12.1 %fusion.13 = bf16[2,1024,768]{2,1,0:T(8,128)(2,1)} fusion(bf16[2,1152,768]{2,0,1:T(2,128)(2,1)} %bitcast.86, bf16[2,1152,1024]{2,1,0:T(8,128)(2,1)} %all-gather.2.cloned.1.call-done, bf16[8,2,1152,128]{3,2,1,0:T(8,128)(2,1)} %all_to_all.16), kind=kOutput, calls=%fused_computation.26 | convolution fusion | flops 3644325888 | bytes 16121856 | tf_op jit(solution)/shard_map/esh,esd->ehd/dot_general | solution.py:61
  375.7 5.5 %all-to-all-done.2 = bf16[2,128,9,768]{3,0,2,1:T(2,128)(2,1)} async-done(((bf16[2,128,9,768]{3,0,2,1:T(2,128)(2,1)}), bf16[2,128,9,768]{3,0,2,1:T(2,128)(2,1)}, u32[]{:S(2)}, u32[]{:S(2)}) %all-to-all-start.2) | async-done | bytes 3538976 | tf_op jit(solution)/shard_map/all_to_all | solution.py:76
  381.2 2.5 copy.117
  383.6 1.0 copy.130
  384.7 2.2 convolution_convert_fusion.1
  (28 shorter events, 3.7 us)
Async XLA Ops:
  7.2 328.3 %copy-start = (bf16[2,1152,768]{2,1,0:T(8,128)(2,1)S(1)}, bf16[2,1152,768]{2,1,0:T(8,128)(2,1)}, u32[]{:S(2)}) copy-start(bf16[2,1152,768]{2,1,0:T(8,128)(2,1)} %param.12) | copy-start | bytes 10616836
  7.2 242.9 %all-reduce.2.cloned.1.call-start = ((), (), s32[]{:S(2)}) async-start(), calls=%async_computation.3 | async-start | bytes 18874368 | tf_op jit(solution)/shard_map/psum | solution.py:45
  18.2 2.6 copy-start.4
  25.9 59.2 %copy-start.6 = (bf16[2,1024,768]{2,1,0:T(8,128)(2,1)S(1)}, bf16[2,1024,768]{2,1,0:T(8,128)(2,1)}, u32[]{:S(2)}) copy-start(bf16[2,1024,768]{2,1,0:T(8,128)(2,1)} %param.17) | copy-start | bytes 9437188
  83.2 1.9 copy-start.3
  91.4 199.3 %all-gather.2.cloned.1.call-start = ((), (), s32[]{:S(2)}) async-start(), calls=%async_computation.4 | async-start | bytes 5308416 | tf_op jit(solution)/shard_map/all_gather | solution.py:51
  290.7 9.1 %copy-start.7 = (bf16[2,768,1024]{2,1,0:T(8,128)(2,1)S(1)}, bf16[2,768,1024]{2,1,0:T(8,128)(2,1)}, u32[]{:S(2)}) copy-start(bf16[2,768,1024]{2,1,0:T(8,128)(2,1)} %param.15) | copy-start | bytes 9437188
  299.7 6.0 %copy-start.1 = (bf16[2,1152,1024]{2,1,0:T(8,128)(2,1)}, bf16[2,1152,1024]{2,1,0:T(8,128)(2,1)S(1)}, u32[]{:S(2)}) copy-start(bf16[2,1152,1024]{2,1,0:T(8,128)(2,1)S(1)} %get-tuple-element.29) | copy-start | bytes 14155780
  299.7 6.4 %copy-start.2 = (bf16[2,1152,1024]{2,1,0:T(8,128)(2,1)}, bf16[2,1152,1024]{2,1,0:T(8,128)(2,1)S(1)}, u32[]{:S(2)}) copy-start(bf16[2,1152,1024]{2,1,0:T(8,128)(2,1)S(1)} %get-tuple-element.28) | copy-start | bytes 14155780
  299.7 6.4 %copy-start.8 = (bf16[2,768,1024]{2,1,0:T(8,128)(2,1)S(1)}, bf16[2,768,1024]{2,1,0:T(8,128)(2,1)}, u32[]{:S(2)}) copy-start(bf16[2,768,1024]{2,1,0:T(8,128)(2,1)} %param.16) | copy-start | bytes 9437188
  326.2 55.0 %all-to-all-start.2 = ((bf16[2,128,9,768]{3,0,2,1:T(2,128)(2,1)}), bf16[2,128,9,768]{3,0,2,1:T(2,128)(2,1)}, u32[]{:S(2)}, u32[]{:S(2)}) async-start(bf16[2,128,9,768]{3,0,2,1:T(2,128)(2,1)} %bitcast.81), calls=%async_computation.2 | async-start | bytes 7077888 | tf_op jit(solution)/shard_map/all_to_all | solution.py:76
  383.6 1.0 copy-start.5
Sparse Core Ops, SparseCore 0:
  91.5 158.5 all-reduce.1
  251.8 38.8 all-gather.1
